TPU v7x, 32 devices: a whole 2x2x4 slice. The times are simulated.
32 devices in a mesh: pipe: 4 (over z), ctx: 2 (over y), dp: 4 (over x, core).
Axes of the slice: x: 2, y: 2, z: 4, core: 2. Of those that a mesh axis runs over, the one named last changes fastest.
Arguments:
- queries: bfloat16 [4, 4, 256, 4096], P('pipe', 'dp', 'ctx'), may hold values from -7 to 7
- key_input: bfloat16 [4, 4, 256, 512], P('pipe', 'dp', 'ctx'), may hold values from -4 to 4
- value_input: bfloat16 [4, 4, 256, 512], P('pipe', 'dp', 'ctx'), may hold values from -6 to 6
- incoming: bfloat16 [4, 4, 256, 4096], P('pipe', 'dp', 'ctx'), may hold values from -6 to 6
- segments: int32 [4, 256], P('dp'), may hold values from 0 to 3, never falling along the last dimension, each value on 1 to 128 neighbouring positions
Outputs:
- query_grad: bfloat16 [4, 4, 256, 4096], P('pipe', 'dp', 'ctx')
- key_grad: bfloat16 [4, 4, 256, 512], P('pipe', 'dp', 'ctx')
- value_grad: bfloat16 [4, 4, 256, 512], P('pipe', 'dp', 'ctx')
- bias_grad: float32 [4, 5120], P('pipe')
Inputs may be any that keep to these rules, and one draw needn't show every extreme that they name: `segments`: tokens of one document are contiguous; every document holds 1 to 128 tokens and one holds exactly 128.
All inputs are finite; a program needn't handle non-finite values.
Results may differ from a plain program's by a relative error of at most 0.009.
Values may be sent and summed in bfloat16 or wider, within the bound.
A program may use at most 64 MiB of HBM per device.

v0:
```python
import math

import jax
import jax.numpy as jnp
from jax import lax
from jax.sharding import PartitionSpec as P

ASKER_STREAMS = 32
SHARED_GROUPS = 4
FEATURE_SIZE = 128
QUERY_PER_KEY = 8


def passed_along(value, axis, steps):
    count = lax.axis_size(axis)
    pairs = [(source, (source + steps) % count) for source in range(count)]
    return lax.ppermute(value, axis, pairs)


def attend(
    queries, key_rows, value_rows, cotangent, query_doc, key_doc, query_pos, key_pos, scaling
):
    scores = (
        jnp.einsum("gqd,kd->gqk", queries, key_rows, preferred_element_type=jnp.float32) * scaling
    )
    visible = (query_doc[:, None] == key_doc[None, :]) & (key_pos[None, :] <= query_pos[:, None])
    scores = jnp.where(visible[None], scores, -1e30)
    row_max = jnp.max(scores, axis=-1, keepdims=True)
    weights = jnp.where(visible[None], jnp.exp(scores - row_max), 0.0)
    probs = weights / jnp.sum(weights, axis=-1, keepdims=True)
    probs_b = probs.astype(jnp.bfloat16)
    attn_out = jnp.einsum("gqk,kd->gqd", probs_b, value_rows, preferred_element_type=jnp.float32)
    dot_out = jnp.sum(cotangent.astype(jnp.float32) * attn_out, axis=-1, keepdims=True)
    grad_prob = jnp.einsum("gqd,kd->gqk", cotangent, value_rows, preferred_element_type=jnp.float32)
    grad_score = (probs * (grad_prob - dot_out) * scaling).astype(jnp.bfloat16)
    asker_derivative = jnp.einsum(
        "gqk,kd->gqd", grad_score, key_rows, preferred_element_type=jnp.float32
    )
    lookup_derivative = jnp.einsum(
        "gqk,gqd->kd", grad_score, queries, preferred_element_type=jnp.float32
    )
    content_derivative = jnp.einsum(
        "gqk,gqd->kd", probs_b, cotangent, preferred_element_type=jnp.float32
    )
    return (asker_derivative, lookup_derivative, content_derivative)


def banded(queries, key_rows, value_rows, cotangent, doc_ids, block_len, scaling):
    length = doc_ids.shape[0]
    blocks = length // block_len
    width = key_rows.shape[1]
    key_pad = jnp.concatenate([jnp.zeros((block_len, width), key_rows.dtype), key_rows], axis=0)
    value_pad = jnp.concatenate(
        [jnp.zeros((block_len, width), value_rows.dtype), value_rows], axis=0
    )
    doc_pad = jnp.concatenate([jnp.full((block_len,), -1, jnp.int32), doc_ids])
    pos_pad = jnp.arange(length + block_len, dtype=jnp.int32) - block_len

    def step(carried, block):
        key_acc, value_acc = carried
        anchor = block * block_len
        query_blk = lax.dynamic_slice_in_dim(queries, anchor, block_len, 1)
        cot_blk = lax.dynamic_slice_in_dim(cotangent, anchor, block_len, 1)
        key_blk = lax.dynamic_slice_in_dim(key_pad, anchor, 2 * block_len, 0)
        value_blk = lax.dynamic_slice_in_dim(value_pad, anchor, 2 * block_len, 0)
        query_doc = lax.dynamic_slice_in_dim(doc_ids, anchor, block_len, 0)
        key_doc = lax.dynamic_slice_in_dim(doc_pad, anchor, 2 * block_len, 0)
        query_pos = anchor + jnp.arange(block_len, dtype=jnp.int32)
        key_pos = lax.dynamic_slice_in_dim(pos_pad, anchor, 2 * block_len, 0)
        asker_derivative, lookup_derivative, content_derivative = attend(
            query_blk, key_blk, value_blk, cot_blk, query_doc, key_doc, query_pos, key_pos, scaling
        )
        key_acc = lax.dynamic_update_slice_in_dim(
            key_acc,
            lax.dynamic_slice_in_dim(key_acc, anchor, 2 * block_len, 0) + lookup_derivative,
            anchor,
            0,
        )
        value_acc = lax.dynamic_update_slice_in_dim(
            value_acc,
            lax.dynamic_slice_in_dim(value_acc, anchor, 2 * block_len, 0) + content_derivative,
            anchor,
            0,
        )
        return ((key_acc, value_acc), asker_derivative)

    start_acc = jnp.zeros((length + block_len, width), jnp.float32)
    (key_acc, value_acc), query_blocks = lax.scan(
        step, (start_acc, start_acc), jnp.arange(blocks, dtype=jnp.int32)
    )
    groups = queries.shape[0]
    asker_derivative = query_blocks.transpose(1, 0, 2, 3).reshape(groups, length, width)
    return (asker_derivative, key_acc[block_len:], value_acc[block_len:])


def body(queries, key_input, value_input, incoming, segments):
    shard_length = queries.shape[2]
    ctx_size = lax.axis_size("ctx")
    reach_dev = min(4, ctx_size - 1)
    block_len = reach_dev * shard_length
    scaling = 1.0 / math.sqrt(FEATURE_SIZE)
    doc_ids = segments[0]
    handed = passed_along(incoming, "pipe", -1)
    query_tok = queries[0, 0].reshape(shard_length, ASKER_STREAMS, FEATURE_SIZE)
    cot_tok = handed[0, 0].reshape(shard_length, ASKER_STREAMS, FEATURE_SIZE)
    key_widened = jnp.repeat(
        key_input[0, 0].reshape(shard_length, SHARED_GROUPS, FEATURE_SIZE), QUERY_PER_KEY, axis=1
    )
    value_widened = jnp.repeat(
        value_input[0, 0].reshape(shard_length, SHARED_GROUPS, FEATURE_SIZE), QUERY_PER_KEY, axis=1
    )
    query_head, key_head, value_head, cot_head = (
        lax.all_to_all(query_tok, "ctx", split_axis=1, concat_axis=0, tiled=True),
        lax.all_to_all(key_widened, "ctx", split_axis=1, concat_axis=0, tiled=True),
        lax.all_to_all(value_widened, "ctx", split_axis=1, concat_axis=0, tiled=True),
        lax.all_to_all(cot_tok, "ctx", split_axis=1, concat_axis=0, tiled=True),
    )

    def per_head(members):
        return banded(
            members[0][None], members[1], members[2], members[3][None], doc_ids, block_len, scaling
        )

    asker_derivative, lookup_derivative, content_derivative = lax.map(
        per_head,
        (
            query_head.transpose(1, 0, 2),
            key_head.transpose(1, 0, 2),
            value_head.transpose(1, 0, 2),
            cot_head.transpose(1, 0, 2),
        ),
    )
    asker_derivative = asker_derivative[:, 0].transpose(1, 0, 2)
    lookup_derivative = lookup_derivative.transpose(1, 0, 2)
    content_derivative = content_derivative.transpose(1, 0, 2)
    query_back, key_backward, value_backward = (
        lax.all_to_all(asker_derivative, "ctx", split_axis=0, concat_axis=1, tiled=True),
        lax.all_to_all(lookup_derivative, "ctx", split_axis=0, concat_axis=1, tiled=True),
        lax.all_to_all(content_derivative, "ctx", split_axis=0, concat_axis=1, tiled=True),
    )
    query_flat = query_back.reshape(shard_length, ASKER_STREAMS * FEATURE_SIZE)
    key_flattened = (
        key_backward.reshape(shard_length, SHARED_GROUPS, QUERY_PER_KEY, FEATURE_SIZE)
        .sum(axis=2)
        .reshape(shard_length, SHARED_GROUPS * FEATURE_SIZE)
    )
    value_flat = (
        value_backward.reshape(shard_length, SHARED_GROUPS, QUERY_PER_KEY, FEATURE_SIZE)
        .sum(axis=2)
        .reshape(shard_length, SHARED_GROUPS * FEATURE_SIZE)
    )
    offset_parts = jnp.concatenate(
        [jnp.sum(query_flat, axis=0), jnp.sum(key_flattened, axis=0), jnp.sum(value_flat, axis=0)]
    )
    offset_overall = lax.psum(offset_parts, ("ctx", "dp"))
    bias_scaled = offset_overall / math.sqrt(lax.axis_size("dp") * shard_length * ctx_size)
    query_grad = query_flat.astype(jnp.bfloat16)[None, None]
    key_grad = key_flattened.astype(jnp.bfloat16)[None, None]
    value_grad = value_flat.astype(jnp.bfloat16)[None, None]
    return (query_grad, key_grad, value_grad, bias_scaled[None])


def solution(mesh):
    return jax.shard_map(
        body,
        mesh=mesh,
        in_specs=(
            P("pipe", "dp", "ctx", None),
            P("pipe", "dp", "ctx", None),
            P("pipe", "dp", "ctx", None),
            P("pipe", "dp", "ctx", None),
            P("dp", None),
        ),
        out_specs=(
            P("pipe", "dp", "ctx", None),
            P("pipe", "dp", "ctx", None),
            P("pipe", "dp", "ctx", None),
            P("pipe", None),
        ),
        check_vma=False,
    )
```

profile of v0, /device:TPU:0, one launch (start us, length us, event | category | flops | bytes accessed | tf_op | source)
XLA Modules:
  0.0 533.1 jit_solution(16299019477271845190)
XLA Ops:
  13.1 8.6 %all-to-all-done.3 = bf16[128,32,128]{2,0,1:T(8,128)(2,1)S(1)} async-done(((bf16[128,32,128]{2,0,1:T(8,128)(2,1)}), bf16[128,32,128]{2,0,1:T(8,128)(2,1)S(1)}, u32[]{:S(2)}, u32[]{:S(2)}) %all-to-all-start.3) | async-done | bytes 1048608 | tf_op jit(solution)/shard_map/all_to_all | solution.py:115
  29.5 10.5 %all-to-all-done.2 = bf16[128,32,128]{2,0,1:T(8,128)(2,1)S(1)} async-done(((bf16[128,32,128]{2,0,1:T(8,128)(2,1)}), bf16[128,32,128]{2,0,1:T(8,128)(2,1)S(1)}, u32[]{:S(2)}, u32[]{:S(2)}) %all-to-all-start.2) | async-done | bytes 1048608 | tf_op jit(solution)/shard_map/all_to_all | solution.py:114
  45.8 10.2 %all-to-all-done = bf16[128,32,128]{2,0,1:T(8,128)(2,1)S(1)} async-done(((bf16[128,32,128]{2,0,1:T(8,128)(2,1)}), bf16[128,32,128]{2,0,1:T(8,128)(2,1)S(1)}, u32[]{:S(2)}, u32[]{:S(2)}) %all-to-all-start) | async-done | bytes 1048608 | tf_op jit(solution)/shard_map/all_to_all | solution.py:113
  65.3 6.8 %all-to-all-done.1 = bf16[128,32,128]{2,0,1:T(8,128)(2,1)} async-done(((bf16[128,32,128]{2,0,1:T(8,128)(2,1)}), bf16[128,32,128]{2,0,1:T(8,128)(2,1)}, u32[]{:S(2)}, u32[]{:S(2)}) %all-to-all-start.1) | async-done | bytes 1048608 | tf_op jit(solution)/shard_map/all_to_all | solution.py:116
  74.9 344.3 %while.46 = (s32[]{:T(128)}, f32[16,1,256,128]{3,0,2,1:T(8,128)}, f32[16,256,128]{2,0,1:T(8,128)}, f32[16,256,128]{2,0,1:T(8,128)}, bf16[16,256,128]{2,1,0:T(8,1...) while((s32[]{:T(128)}, f32[16,1,256,128]{3,0,2,1:T(8,128)}, ...), condition=%wide.region_6.7_spmd, body=%wide.region_0.6_spmd.sunk | while | flops 51626120 | bytes 4455093 | solution.py:124
  75.9 6.4 %while.47 = (s32[]{:T(128)}, f32[384,128]{1,0:T(8,128)S(1)}, f32[384,128]{1,0:T(8,128)S(1)}, f32[2,1,128,128]{3,2,1,0:T(8,128)S(1)}, s32[2]{0:T(128)S(1)}, /*ind...) while((s32[]{:T(128)}, f32[384,128]{1,0:T(8,128)S(1)}, ...), condition=%wide.region_5.5_spmd, body=%wide.region_1.4_spmd.sunk | while | flops 51625736 | bytes 1894712 | solution.py:88
  97.4 6.4 %while.47 = (s32[]{:T(128)}, f32[384,128]{1,0:T(8,128)S(1)}, f32[384,128]{1,0:T(8,128)S(1)}, f32[2,1,128,128]{3,2,1,0:T(8,128)S(1)}, s32[2]{0:T(128)S(1)}, /*ind...) while((s32[]{:T(128)}, f32[384,128]{1,0:T(8,128)S(1)}, ...), condition=%wide.region_5.5_spmd, body=%wide.region_1.4_spmd.sunk | while | flops 51625736 | bytes 1894712 | solution.py:88
  118.9 6.4 %while.47 = (s32[]{:T(128)}, f32[384,128]{1,0:T(8,128)S(1)}, f32[384,128]{1,0:T(8,128)S(1)}, f32[2,1,128,128]{3,2,1,0:T(8,128)S(1)}, s32[2]{0:T(128)S(1)}, /*ind...) while((s32[]{:T(128)}, f32[384,128]{1,0:T(8,128)S(1)}, ...), condition=%wide.region_5.5_spmd, body=%wide.region_1.4_spmd.sunk | while | flops 51625736 | bytes 1894712 | solution.py:88
  140.4 6.4 %while.47 = (s32[]{:T(128)}, f32[384,128]{1,0:T(8,128)S(1)}, f32[384,128]{1,0:T(8,128)S(1)}, f32[2,1,128,128]{3,2,1,0:T(8,128)S(1)}, s32[2]{0:T(128)S(1)}, /*ind...) while((s32[]{:T(128)}, f32[384,128]{1,0:T(8,128)S(1)}, ...), condition=%wide.region_5.5_spmd, body=%wide.region_1.4_spmd.sunk | while | flops 51625736 | bytes 1894712 | solution.py:88
  161.9 6.4 %while.47 = (s32[]{:T(128)}, f32[384,128]{1,0:T(8,128)S(1)}, f32[384,128]{1,0:T(8,128)S(1)}, f32[2,1,128,128]{3,2,1,0:T(8,128)S(1)}, s32[2]{0:T(128)S(1)}, /*ind...) while((s32[]{:T(128)}, f32[384,128]{1,0:T(8,128)S(1)}, ...), condition=%wide.region_5.5_spmd, body=%wide.region_1.4_spmd.sunk | while | flops 51625736 | bytes 1894712 | solution.py:88
  183.4 6.4 %while.47 = (s32[]{:T(128)}, f32[384,128]{1,0:T(8,128)S(1)}, f32[384,128]{1,0:T(8,128)S(1)}, f32[2,1,128,128]{3,2,1,0:T(8,128)S(1)}, s32[2]{0:T(128)S(1)}, /*ind...) while((s32[]{:T(128)}, f32[384,128]{1,0:T(8,128)S(1)}, ...), condition=%wide.region_5.5_spmd, body=%wide.region_1.4_spmd.sunk | while | flops 51625736 | bytes 1894712 | solution.py:88
  204.9 6.4 %while.47 = (s32[]{:T(128)}, f32[384,128]{1,0:T(8,128)S(1)}, f32[384,128]{1,0:T(8,128)S(1)}, f32[2,1,128,128]{3,2,1,0:T(8,128)S(1)}, s32[2]{0:T(128)S(1)}, /*ind...) while((s32[]{:T(128)}, f32[384,128]{1,0:T(8,128)S(1)}, ...), condition=%wide.region_5.5_spmd, body=%wide.region_1.4_spmd.sunk | while | flops 51625736 | bytes 1894712 | solution.py:88
  226.4 6.4 %while.47 = (s32[]{:T(128)}, f32[384,128]{1,0:T(8,128)S(1)}, f32[384,128]{1,0:T(8,128)S(1)}, f32[2,1,128,128]{3,2,1,0:T(8,128)S(1)}, s32[2]{0:T(128)S(1)}, /*ind...) while((s32[]{:T(128)}, f32[384,128]{1,0:T(8,128)S(1)}, ...), condition=%wide.region_5.5_spmd, body=%wide.region_1.4_spmd.sunk | while | flops 51625736 | bytes 1894712 | solution.py:88
  247.9 6.4 %while.47 = (s32[]{:T(128)}, f32[384,128]{1,0:T(8,128)S(1)}, f32[384,128]{1,0:T(8,128)S(1)}, f32[2,1,128,128]{3,2,1,0:T(8,128)S(1)}, s32[2]{0:T(128)S(1)}, /*ind...) while((s32[]{:T(128)}, f32[384,128]{1,0:T(8,128)S(1)}, ...), condition=%wide.region_5.5_spmd, body=%wide.region_1.4_spmd.sunk | while | flops 51625736 | bytes 1894712 | solution.py:88
  254.3 4.7 dynamic_update_slice.41
  269.4 6.4 %while.47 = (s32[]{:T(128)}, f32[384,128]{1,0:T(8,128)S(1)}, f32[384,128]{1,0:T(8,128)S(1)}, f32[2,1,128,128]{3,2,1,0:T(8,128)S(1)}, s32[2]{0:T(128)S(1)}, /*ind...) while((s32[]{:T(128)}, f32[384,128]{1,0:T(8,128)S(1)}, ...), condition=%wide.region_5.5_spmd, body=%wide.region_1.4_spmd.sunk | while | flops 51625736 | bytes 1894712 | solution.py:88
  275.8 4.7 dynamic_update_slice.41
  290.9 6.4 %while.47 = (s32[]{:T(128)}, f32[384,128]{1,0:T(8,128)S(1)}, f32[384,128]{1,0:T(8,128)S(1)}, f32[2,1,128,128]{3,2,1,0:T(8,128)S(1)}, s32[2]{0:T(128)S(1)}, /*ind...) while((s32[]{:T(128)}, f32[384,128]{1,0:T(8,128)S(1)}, ...), condition=%wide.region_5.5_spmd, body=%wide.region_1.4_spmd.sunk | while | flops 51625736 | bytes 1894712 | solution.py:88
  297.4 4.7 dynamic_update_slice.41
  312.5 6.4 %while.47 = (s32[]{:T(128)}, f32[384,128]{1,0:T(8,128)S(1)}, f32[384,128]{1,0:T(8,128)S(1)}, f32[2,1,128,128]{3,2,1,0:T(8,128)S(1)}, s32[2]{0:T(128)S(1)}, /*ind...) while((s32[]{:T(128)}, f32[384,128]{1,0:T(8,128)S(1)}, ...), condition=%wide.region_5.5_spmd, body=%wide.region_1.4_spmd.sunk | while | flops 51625736 | bytes 1894712 | solution.py:88
  318.9 4.7 dynamic_update_slice.41
  334.0 6.4 %while.47 = (s32[]{:T(128)}, f32[384,128]{1,0:T(8,128)S(1)}, f32[384,128]{1,0:T(8,128)S(1)}, f32[2,1,128,128]{3,2,1,0:T(8,128)S(1)}, s32[2]{0:T(128)S(1)}, /*ind...) while((s32[]{:T(128)}, f32[384,128]{1,0:T(8,128)S(1)}, ...), condition=%wide.region_5.5_spmd, body=%wide.region_1.4_spmd.sunk | while | flops 51625736 | bytes 1894712 | solution.py:88
  340.4 4.7 dynamic_update_slice.41
  355.6 6.4 %while.47 = (s32[]{:T(128)}, f32[384,128]{1,0:T(8,128)S(1)}, f32[384,128]{1,0:T(8,128)S(1)}, f32[2,1,128,128]{3,2,1,0:T(8,128)S(1)}, s32[2]{0:T(128)S(1)}, /*ind...) while((s32[]{:T(128)}, f32[384,128]{1,0:T(8,128)S(1)}, ...), condition=%wide.region_5.5_spmd, body=%wide.region_1.4_spmd.sunk | while | flops 51625736 | bytes 1894712 | solution.py:88
  362.0 4.7 dynamic_update_slice.41
  377.1 6.4 %while.47 = (s32[]{:T(128)}, f32[384,128]{1,0:T(8,128)S(1)}, f32[384,128]{1,0:T(8,128)S(1)}, f32[2,1,128,128]{3,2,1,0:T(8,128)S(1)}, s32[2]{0:T(128)S(1)}, /*ind...) while((s32[]{:T(128)}, f32[384,128]{1,0:T(8,128)S(1)}, ...), condition=%wide.region_5.5_spmd, body=%wide.region_1.4_spmd.sunk | while | flops 51625736 | bytes 1894712 | solution.py:88
  398.7 6.4 %while.47 = (s32[]{:T(128)}, f32[384,128]{1,0:T(8,128)S(1)}, f32[384,128]{1,0:T(8,128)S(1)}, f32[2,1,128,128]{3,2,1,0:T(8,128)S(1)}, s32[2]{0:T(128)S(1)}, /*ind...) while((s32[]{:T(128)}, f32[384,128]{1,0:T(8,128)S(1)}, ...), condition=%wide.region_5.5_spmd, body=%wide.region_1.4_spmd.sunk | while | flops 51625736 | bytes 1894712 | solution.py:88
  419.1 25.8 %all_to_all.117 = f32[256,16,128]{2,1,0:T(8,128)S(1)} all-to-all(f32[256,16,128]{2,1,0:T(8,128)} %bitcast.139), channel_id=1, replica_groups=mesh['pipe'=4,'ctx'=2,'dp'=4] {'ctx'}, dimensions={0} | all-to-all | bytes 4194304 | tf_op jit(solution)/shard_map/all_to_all | solution.py:139
  444.9 24.4 %all_to_all.118 = f32[256,16,128]{2,1,0:T(8,128)} all-to-all(f32[256,16,128]{2,1,0:T(8,128)S(1)} %bitcast.140), channel_id=1, replica_groups=mesh['pipe'=4,'ctx'=2,'dp'=4] {'ctx'}, dimensions={0} | all-to-all | bytes 4194304 | tf_op jit(solution)/shard_map/all_to_all | solution.py:138
  469.3 4.8 all-to-all-start.4
  476.1 18.2 %all-to-all-done.4 = f32[256,16,128]{2,1,0:T(8,128)} async-done(((f32[256,16,128]{2,1,0:T(8,128)}), f32[256,16,128]{2,1,0:T(8,128)}, u32[]{:S(2)}, u32[]{:S(2)}) %all-to-all-start.4) | async-done | bytes 2097184 | tf_op jit(solution)/shard_map/all_to_all | solution.py:137
  496.0 22.5 %psum.7 = f32[5120]{0:T(1024)S(1)} all-reduce(f32[5120]{0:T(1024)S(1)} %pad_maximum_fusion), channel_id=1, replica_groups=mesh['pipe'=4,'ctx'=2,'dp'=4] {'ctx','dp'}, use_global_device_ids=true, to_apply=%region_14.15 | all-reduce | flops 5120 | bytes 40960 | tf_op jit(solution)/shard_map/psum | solution.py:155
  (685 shorter events, 348.4 us)
Async XLA Ops:
  0.6 6.6 %copy-start.1 = (bf16[1,1,128,4096]{3,2,1,0:T(8,128)(2,1)S(1)}, bf16[1,1,128,4096]{3,2,1,0:T(8,128)(2,1)}, u32[]{:S(2)}) copy-start(bf16[1,1,128,4096]{3,2,1,0:T(8,128)(2,1)} %param.12) | copy-start | bytes 3145732
  2.9 10.1 %copy-start.2 = (bf16[1,1,128,512]{3,2,1,0:T(8,128)(2,1)S(1)}, bf16[1,1,128,512]{3,2,1,0:T(8,128)(2,1)}, u32[]{:S(2)}) copy-start(bf16[1,1,128,512]{3,2,1,0:T(8,128)(2,1)} %param.10) | copy-start | bytes 393220
  2.9 18.8 %all-to-all-start.3 = ((bf16[128,32,128]{2,0,1:T(8,128)(2,1)}), bf16[128,32,128]{2,0,1:T(8,128)(2,1)S(1)}, u32[]{:S(2)}, u32[]{:S(2)}) async-start(bf16[128,32,128]{2,0,1:T(8,128)(2,1)} %bitcast.28), calls=%async_computation.3 | async-start | bytes 2097152 | tf_op jit(solution)/shard_map/all_to_all | solution.py:115
  8.6 34.9 %collective-permute-start = (bf16[1,1,128,4096]{2,3,1,0:T(8,128)(2,1)}, bf16[1,1,128,4096]{2,3,1,0:T(8,128)(2,1)}, u32[]{:S(2)}, u32[]{:S(2)}) collective-permute-start(bf16[1,1,128,4096]{2,3,1,0:T(8,128)(2,1)} %copy.72), channel_id=1, source_target_pairs={{0,24},{8,0},{16,8},{24,16},{1,25},{9,1},{17,9},{25,17},{2,26},{10... | collective-permute-start | bytes 3145736 | tf_op jit(solution)/shard_map/ppermute | solution.py:17
  22.9 17.0 %all-to-all-start.2 = ((bf16[128,32,128]{2,0,1:T(8,128)(2,1)}), bf16[128,32,128]{2,0,1:T(8,128)(2,1)S(1)}, u32[]{:S(2)}, u32[]{:S(2)}) async-start(bf16[128,32,128]{2,0,1:T(8,128)(2,1)} %bitcast.22), calls=%async_computation.2 | async-start | bytes 2097152 | tf_op jit(solution)/shard_map/all_to_all | solution.py:114
  39.9 16.1 %all-to-all-start = ((bf16[128,32,128]{2,0,1:T(8,128)(2,1)}), bf16[128,32,128]{2,0,1:T(8,128)(2,1)S(1)}, u32[]{:S(2)}, u32[]{:S(2)}) async-start(bf16[128,32,128]{2,0,1:T(8,128)(2,1)} %copy.69), calls=%async_computation | async-start | bytes 2097152 | tf_op jit(solution)/shard_map/all_to_all | solution.py:113
  56.0 16.1 %all-to-all-start.1 = ((bf16[128,32,128]{2,0,1:T(8,128)(2,1)}), bf16[128,32,128]{2,0,1:T(8,128)(2,1)}, u32[]{:S(2)}, u32[]{:S(2)}) async-start(bf16[128,32,128]{2,0,1:T(8,128)(2,1)} %copy.73), calls=%async_computation.1 | async-start | bytes 2097152 | tf_op jit(solution)/shard_map/all_to_all | solution.py:116
  72.1 2.7 copy-start.3
  419.1 25.8 %copy-start = (f32[16,256,128]{2,0,1:T(8,128)S(1)}, f32[16,256,128]{2,0,1:T(8,128)}, u32[]{:S(2)}) copy-start(f32[16,256,128]{2,0,1:T(8,128)} %get-tuple-element.554) | copy-start | bytes 6291460
  469.3 24.9 %all-to-all-start.4 = ((f32[256,16,128]{2,1,0:T(8,128)}), f32[256,16,128]{2,1,0:T(8,128)}, u32[]{:S(2)}, u32[]{:S(2)}) async-start(f32[256,16,128]{2,1,0:T(8,128)} %bitcast.141), calls=%async_computation.4 | async-start | bytes 4194304 | tf_op jit(solution)/shard_map/all_to_all | solution.py:137
where the time goes:
time: 538 us; the launch traced here: 533 us
  local copies, waits for them, and re-layouts  292 us (54%)
  blocking collectives  72.7 us (14%)
  waiting for transfers between devices  54.2 us (10%)
  matrix products  46.7 us (9%)
  starting transfers between devices  25.2 us (5%)
  loops' own time  23.7 us (4%)
  other arithmetic  17.3 us (3%)
    dynamic_update_slice x48, local copies, waits for them, and re-layouts, body(): lax.map(per_head, (query_head.transpose(1, 0, 2), key_head.transpose(1, 0...  225 us
    all_to_all x1, blocking collectives, body(): lax.all_to_all(content_derivative, 'ctx', split_axis=0, concat_axis=1, ti...  25.8 us
    all_to_all x1, blocking collectives, body(): lax.all_to_all(lookup_derivative, 'ctx', split_axis=0, concat_axis=1, til...  24.4 us
    psum x1, blocking collectives, body(): offset_overall = lax.psum(offset_parts, ('ctx', 'dp'))  22.5 us
    another operation x16, loops' own time, banded(): lax.scan(step, (start_acc, start_acc), jnp.arange(blocks, dtype=jnp.int32))  22.3 us
    dynamic_slice x32, local copies, waits for them, and re-layouts, banded(): lax.scan(step, (start_acc, start_acc), jnp.arange(blocks, dtype=jnp.int32))  18.8 us
    all_to_all x1, waiting for transfers between devices, body(): lax.all_to_all(asker_derivative, 'ctx', split_axis=0, concat_axis=1, tile...  18.2 us
    squeeze x16, local copies, waits for them, and re-layouts, body(): lax.map(per_head, (query_head.transpose(1, 0, 2), key_head.transpose(1, 0...  14.2 us
  transfers between devices with their start and end apart: 6, of which 5 were waited for; matrix products, arithmetic and copies ran while one was open for 3% of the time, Pallas kernels for 0%

commit v1 on v0

v1 whole, which is shorter than its diff:
```python
import functools
import math

import jax
import jax.numpy as jnp
from jax import lax
from jax.experimental import pallas as pl
from jax.experimental.pallas import tpu as pltpu
from jax.sharding import PartitionSpec as P

ASKER_STREAMS = 32
SHARED_GROUPS = 4
FEATURE_SIZE = 128
QUERY_PER_KEY = 8
HALF = 4
BIAS_ROWS = 16
MESH = pl.DeviceIdType.MESH
F32 = jnp.float32
BF16 = jnp.bfloat16


def dot(a, b, a_dim, b_dim):
    return lax.dot_general(a, b, (((a_dim,), (b_dim,)), ((), ())), preferred_element_type=F32)


def kernel(
    sizes, in_kernel_sum,
    q_hbm, k_hbm, v_hbm, inc_hbm, seg_hbm,
    dq_hbm, dk_hbm, dv_hbm, bias_hbm,
    q_rows, cot_rows, keys, values, seg, mask_add, probs, acc, dq_rows,
    back_out, back_in, bias_mine, bias_in, dk_out, dv_out, bias_out,
    q_sem, cot_send, cot_recv, own_sem, halo_send, halo_recv, seg_sem,
    back_send, back_recv, bias_send, bias_recv, dq_sem, out_sem,
):
    pipe, ctx, dp, reach = sizes
    rows = q_hbm.shape[0]
    width = FEATURE_SIZE
    window = (reach + 1) * rows
    length = seg_hbm.shape[1]
    scaling = 1.0 / math.sqrt(FEATURE_SIZE)
    my_pipe, my_ctx, my_dp = lax.axis_index("pipe"), lax.axis_index("ctx"), lax.axis_index("dp")

    below = lax.rem(my_pipe + pipe - 1, pipe)
    above = lax.rem(my_pipe + 1, pipe)
    offsets = [(d, c) for d in range(dp) for c in range(ctx) if (d, c) != (0, 0)]

    def peer(d, c):
        return {"dp": lax.rem(my_dp + d, dp), "ctx": lax.rem(my_ctx + c, ctx)}

    def ahead(r):
        return {"ctx": lax.rem(my_ctx + r, ctx)}

    def behind(r):
        return {"ctx": lax.rem(my_ctx + ctx - r, ctx)}

    def columns(index):
        return pl.ds(pl.multiple_of(index * width, width), width)

    def head_rows(index):
        return pl.ds(pl.multiple_of(index * rows, rows), rows)

    def cot_copy(h):
        return pltpu.make_async_remote_copy(
            src_ref=inc_hbm.at[:, columns(h)], dst_ref=cot_rows.at[head_rows(h)],
            send_sem=cot_send.at[h], recv_sem=cot_recv.at[h],
            device_id={"pipe": below}, device_id_type=MESH,
        )

    def q_copy(h):
        return pltpu.make_async_copy(q_hbm.at[:, columns(h)], q_rows.at[head_rows(h)], q_sem.at[h])

    def dq_copy(h):
        return pltpu.make_async_copy(dq_rows.at[head_rows(h)], dq_hbm.at[:, columns(h)], dq_sem.at[h])

    def halo_copy(i, r):
        src, dst = (k_hbm, keys) if i == 0 else (v_hbm, values)
        return pltpu.make_async_remote_copy(
            src_ref=src, dst_ref=dst.at[pl.ds((reach - r) * rows, rows)],
            send_sem=halo_send.at[i, r - 1], recv_sem=halo_recv.at[i, r - 1],
            device_id=ahead(r), device_id_type=MESH,
        )

    def back_copy(g, r):
        return pltpu.make_async_remote_copy(
            src_ref=back_out.at[g, r - 1], dst_ref=back_in.at[g, r - 1],
            send_sem=back_send.at[g, r - 1], recv_sem=back_recv.at[g, r - 1],
            device_id=behind(r), device_id_type=MESH,
        )

    def bias_copy(g, i):
        return pltpu.make_async_remote_copy(
            src_ref=bias_mine.at[g], dst_ref=bias_in.at[i, g],
            send_sem=bias_send.at[i, g], recv_sem=bias_recv.at[i, g],
            device_id=peer(*offsets[i]), device_id_type=MESH,
        )

    own_copies = [
        pltpu.make_async_copy(k_hbm, keys.at[pl.ds(reach * rows, rows)], own_sem.at[0]),
        pltpu.make_async_copy(v_hbm, values.at[pl.ds(reach * rows, rows)], own_sem.at[1]),
    ]
    seg_copy = pltpu.make_async_copy(seg_hbm, seg, seg_sem)

    barrier = pltpu.get_barrier_semaphore()
    greeted = [{"pipe": below}, {"pipe": above}]
    if in_kernel_sum:
        greeted += [peer(d, c) for d, c in offsets]
    else:
        greeted += [ahead(r) for r in range(1, reach + 1)] + [behind(r) for r in range(1, reach + 1)]
    for other in greeted:
        pl.semaphore_signal(barrier, inc=1, device_id=other, device_id_type=MESH)
    seg_copy.start()
    for copy in own_copies:
        copy.start()

    @pl.loop(0, ASKER_STREAMS)
    def _(h):
        q_copy(h).start()

    pl.semaphore_wait(barrier, len(greeted))

    for r in range(1, reach + 1):
        for i in range(2):
            halo_copy(i, r).start()

    @pl.loop(0, ASKER_STREAMS)
    def _(h):
        cot_copy(h).start()

    seg_copy.wait()
    query_doc = seg[:, pl.ds(pl.multiple_of(my_ctx * rows, rows), rows)].astype(F32)
    query_pos = lax.broadcasted_iota(jnp.int32, (rows, rows), 1) + my_ctx * rows
    for b in range(reach + 1):
        r = reach - b
        block = lax.rem(my_ctx + ctx - r, ctx)
        key_doc = seg[:, pl.ds(pl.multiple_of(block * rows, rows), rows)].astype(F32)
        key_doc = jnp.broadcast_to(key_doc, (rows, rows)).T
        key_pos = lax.broadcasted_iota(jnp.int32, (rows, rows), 0) + (my_ctx - r) * rows
        visible = (key_doc == query_doc) & (key_pos <= query_pos) & (key_pos >= 0)
        mask_add[pl.ds(b * rows, rows), :] = jnp.where(visible, 0.0, -1e30)

    @pl.loop(0, ASKER_STREAMS)
    def _(h):
        q_copy(h).wait()

    for copy in own_copies:
        copy.wait()
    for r in range(1, reach + 1):
        for i in range(2):
            halo_copy(i, r).wait_recv()

    to_exp2 = scaling * math.log2(math.e)

    @pl.loop(0, SHARED_GROUPS)
    def _(g):
        key_block = keys[:, columns(g)]
        for i in range(QUERY_PER_KEY):
            h = g * QUERY_PER_KEY + i
            scores = dot(key_block, q_rows[head_rows(h), :], 1, 1) * to_exp2 + mask_add[...]
            weights = jnp.exp2(scores - jnp.max(scores, axis=0, keepdims=True))
            probs[h] = weights * (1.0 / jnp.sum(weights, axis=0, keepdims=True))

    @pl.loop(0, SHARED_GROUPS)
    def _(g):
        key_block = keys[:, columns(g)]
        value_block = values[:, columns(g)]
        for half in range(QUERY_PER_KEY // HALF):
            first = g * QUERY_PER_KEY + half * HALF
            grads, probs_b = [], []
            for i in range(HALF):
                h = first + i
                cot_copy(h).wait_recv()
                p = probs[h]
                pb = p.astype(BF16)
                grad_prob = dot(value_block, cot_rows[head_rows(h), :], 1, 1)
                dot_out = jnp.sum(pb.astype(F32) * grad_prob, axis=0, keepdims=True)
                grads.append((p * (grad_prob - dot_out) * scaling).astype(BF16))
                probs_b.append(pb)
            grads = jnp.concatenate(grads, axis=1)
            probs_b = jnp.concatenate(probs_b, axis=1)
            these = pl.ds(pl.multiple_of(first * rows, rows), HALF * rows)
            dk = dot(grads, q_rows[these, :], 1, 0)
            dv = dot(probs_b, cot_rows[these, :], 1, 0)
            if half:
                dk = acc[g, 0] + dk
                dv = acc[g, 1] + dv
            acc[g, 0] = dk
            acc[g, 1] = dv
            if half == QUERY_PER_KEY // HALF - 1:
                for r in range(1, reach + 1):
                    part = slice((reach - r) * rows, (reach - r + 1) * rows)
                    back_out[g, r - 1, 0] = dk[part].astype(BF16)
                    back_out[g, r - 1, 1] = dv[part].astype(BF16)
                    back_copy(g, r).start()
                bias_mine[g, 8:9, :] = jnp.sum(dk, axis=0, keepdims=True)
                bias_mine[g, 9:10, :] = jnp.sum(dv, axis=0, keepdims=True)
            dq = dot(grads, key_block, 0, 0)
            dq_rows[these, :] = dq.astype(BF16)
            for i in range(HALF):
                row = half * HALF + i
                bias_mine[g, row : row + 1, :] = jnp.sum(
                    dq[i * rows : (i + 1) * rows], axis=0, keepdims=True
                )
                dq_copy(first + i).start()
        if in_kernel_sum:
            for i in range(len(offsets)):
                bias_copy(g, i).start()

    for g in range(SHARED_GROUPS):
        part = pl.ds(g * width, width)
        dk = acc[g, 0, pl.ds(reach * rows, rows), :]
        dv = acc[g, 1, pl.ds(reach * rows, rows), :]
        for r in range(1, reach + 1):
            back_copy(g, r).wait_recv()
            dk = dk + back_in[g, r - 1, 0].astype(F32)
            dv = dv + back_in[g, r - 1, 1].astype(F32)
        dk_out[:, part] = dk.astype(BF16)
        dv_out[:, part] = dv.astype(BF16)
    outs = [
        pltpu.make_async_copy(dk_out, dk_hbm, out_sem.at[0]),
        pltpu.make_async_copy(dv_out, dv_hbm, out_sem.at[1]),
        pltpu.make_async_copy(bias_out, bias_hbm, out_sem.at[2]),
    ]
    outs[0].start()
    outs[1].start()

    bias_scale = 1.0 / math.sqrt(dp * length)
    for g in range(SHARED_GROUPS):
        total = bias_mine[g]
        if in_kernel_sum:
            for i in range(len(offsets)):
                bias_copy(g, i).wait_recv()
                total = total + bias_in[i, g]
        total = total * bias_scale
        for i in range(QUERY_PER_KEY):
            bias_out[:, pl.ds((g * QUERY_PER_KEY + i) * width, width)] = total[i : i + 1, :]
        bias_out[:, pl.ds((ASKER_STREAMS + g) * width, width)] = total[8:9, :]
        bias_out[:, pl.ds((ASKER_STREAMS + SHARED_GROUPS + g) * width, width)] = total[9:10, :]
    outs[2].start()

    for r in range(1, reach + 1):
        for i in range(2):
            halo_copy(i, r).wait_send()
        for g in range(SHARED_GROUPS):
            back_copy(g, r).wait_send()
    if in_kernel_sum:
        for i in range(len(offsets)):
            for g in range(SHARED_GROUPS):
                bias_copy(g, i).wait_send()

    @pl.loop(0, ASKER_STREAMS)
    def _(h):
        cot_copy(h).wait_send()
        dq_copy(h).wait()

    for copy in outs:
        copy.wait()


def body(pipe, ctx, dp, queries, key_input, value_input, incoming, segments):
    rows = queries.shape[2]
    length = segments.shape[1]
    reach = min(4, ctx - 1)
    window = (reach + 1) * rows
    in_kernel_sum = dp * ctx <= 16
    peers = dp * ctx - 1 if in_kernel_sum else 1
    q_width = ASKER_STREAMS * FEATURE_SIZE
    kv_width = SHARED_GROUPS * FEATURE_SIZE
    dma = pltpu.SemaphoreType.DMA
    dq, dk, dv, bias = pl.pallas_call(
        functools.partial(kernel, (pipe, ctx, dp, reach), in_kernel_sum),
        out_shape=(
            jax.ShapeDtypeStruct((rows, q_width), BF16),
            jax.ShapeDtypeStruct((rows, kv_width), BF16),
            jax.ShapeDtypeStruct((rows, kv_width), BF16),
            jax.ShapeDtypeStruct((1, q_width + 2 * kv_width), F32),
        ),
        in_specs=[pl.BlockSpec(memory_space=pl.ANY)] * 5,
        out_specs=[pl.BlockSpec(memory_space=pl.ANY)] * 4,
        scratch_shapes=[
            pltpu.VMEM((ASKER_STREAMS * rows, FEATURE_SIZE), BF16),
            pltpu.VMEM((ASKER_STREAMS * rows, FEATURE_SIZE), BF16),
            pltpu.VMEM((window, kv_width), BF16),
            pltpu.VMEM((window, kv_width), BF16),
            pltpu.VMEM((1, length), jnp.int32),
            pltpu.VMEM((window, rows), F32),
            pltpu.VMEM((ASKER_STREAMS, window, rows), F32),
            pltpu.VMEM((SHARED_GROUPS, 2, window, FEATURE_SIZE), F32),
            pltpu.VMEM((ASKER_STREAMS * rows, FEATURE_SIZE), BF16),
            pltpu.VMEM((SHARED_GROUPS, reach, 2, rows, FEATURE_SIZE), BF16),
            pltpu.VMEM((SHARED_GROUPS, reach, 2, rows, FEATURE_SIZE), BF16),
            pltpu.VMEM((SHARED_GROUPS, BIAS_ROWS, FEATURE_SIZE), F32),
            pltpu.VMEM((peers, SHARED_GROUPS, BIAS_ROWS, FEATURE_SIZE), F32),
            pltpu.VMEM((rows, kv_width), BF16),
            pltpu.VMEM((rows, kv_width), BF16),
            pltpu.VMEM((1, q_width + 2 * kv_width), F32),
            dma((ASKER_STREAMS,)),
            dma((ASKER_STREAMS,)),
            dma((ASKER_STREAMS,)),
            dma((2,)),
            dma((2, reach)),
            dma((2, reach)),
            dma,
            dma((SHARED_GROUPS, reach)),
            dma((SHARED_GROUPS, reach)),
            dma((peers, SHARED_GROUPS)),
            dma((peers, SHARED_GROUPS)),
            dma((ASKER_STREAMS,)),
            dma((3,)),
        ],
        compiler_params=pltpu.CompilerParams(
            collective_id=0, has_side_effects=True, vmem_limit_bytes=48 * 1024 * 1024
        ),
    )(queries[0, 0], key_input[0, 0], value_input[0, 0], incoming[0, 0], segments)
    if not in_kernel_sum:
        bias = lax.psum(bias, ("ctx", "dp"))
    return dq[None, None], dk[None, None], dv[None, None], bias


def solution(mesh):
    tokens = P("pipe", "dp", "ctx", None)
    return jax.shard_map(
        functools.partial(body, mesh.shape["pipe"], mesh.shape["ctx"], mesh.shape["dp"]),
        mesh=mesh,
        in_specs=(tokens, tokens, tokens, tokens, P("dp", None)),
        out_specs=(tokens, tokens, tokens, P("pipe", None)),
        check_vma=False,
    )
```

time: 538 us -> 43.6 us (0.08)
  local copies, waits for them, and re-layouts: 292 us -> 7.82 us
  blocking collectives: 72.7 us -> 0 us
  waiting for transfers between devices: 54.2 us -> 0 us
  matrix products: 46.7 us -> 0 us
  Pallas kernels: 0 us -> 34.8 us
  starting transfers between devices: 25.2 us -> 0 us
  loops' own time: 23.7 us -> 0 us
  other arithmetic: 17.3 us -> 0 us
    dynamic_update_slice x48 -> x0, local copies, waits for them, and re-layouts: 225 us -> none  [body(): lax.map(per_head, (query_head.transpose(1, 0, 2), key_head.transpose(1, 0...]
    all_to_all x5 -> x0, waiting for transfers between devices: 54.2 us -> none  [the longest x1 18.2 us: body(): lax.all_to_all(asker_derivative, 'ctx', split_axis=0, concat_axis=1, tile...]
    all_to_all x2 -> x0, blocking collectives: 50.1 us -> none  [the longest x1 25.8 us: body(): lax.all_to_all(content_derivative, 'ctx', split_axis=0, concat_axis=1, ti...]
    dot_general x192 -> x0, matrix products: 46.7 us -> none  [the longest x32 10.1 us: attend(): jnp.einsum('gqk,gqd->kd', probs_b, cotangent, preferred_element_type=jnp....]
    pallas_call x0 -> x1, Pallas kernels: none -> 34.8 us  [body(): pl.pallas_call(functools.partial(kernel, (pipe, ctx, dp, reach), in_kerne...]
    dynamic_slice x160 -> x0, local copies, waits for them, and re-layouts: 26.5 us -> none  [the longest x32 18.8 us: banded(): lax.scan(step, (start_acc, start_acc), jnp.arange(blocks, dtype=jnp.int32))]
    another operation x17 -> x0, loops' own time: 23.7 us -> none  [the longest x16 22.3 us: banded(): lax.scan(step, (start_acc, start_acc), jnp.arange(blocks, dtype=jnp.int32))]
    psum x1 -> x0, blocking collectives: 22.5 us -> none  [body(): offset_overall = lax.psum(offset_parts, ('ctx', 'dp'))]
  transfers between devices with their start and end apart: 6 -> 0, of which waited for: 5 -> 0; matrix products, arithmetic and copies ran while one was open for 3% -> 0% of each run, Pallas kernels for 0% -> 0%
where the time goes in v1:
time: 43.6 us; the launch traced here: 43.3 us
  Pallas kernels  34.8 us (80%)
  local copies, waits for them, and re-layouts  7.82 us (18%)
  between operations  0.65 us (1%)
    pallas_call x1, Pallas kernels, body(): pl.pallas_call(functools.partial(kernel, (pipe, ctx, dp, reach), in_kerne...  34.8 us
    unnamed x14, local copies, waits for them, and re-layouts  7.82 us

profile of v1, /device:TPU:0, one launch (start us, length us, event | category | flops | bytes accessed | tf_op | source)
XLA Modules:
  0.0 43.3 jit_solution(3038340425031538279)
XLA Ops:
  0.6 0.0 copy-start.4
  0.6 0.7 %copy-done.4 = s32[1,256]{1,0:T(1,128)S(1)} copy-done((s32[1,256]{1,0:T(1,128)S(1)}, s32[1,256]{1,0:T(1,128)}, u32[]{:S(2)}) %copy-start.4) | copy-done | bytes 1048
  1.3 0.0 copy-start
  1.3 1.2 %copy-done = bf16[1,1,128,4096]{3,2,1,0:T(8,128)(2,1)S(1)} copy-done((bf16[1,1,128,4096]{3,2,1,0:T(8,128)(2,1)S(1)}, bf16[1,1,128,4096]{3,2,1,0:T(8,128)(2,1)}, u32[]{:S(2)}) %copy-start) | copy-done | bytes 1048600
  2.5 0.0 copy-start.1
  2.5 1.2 %copy-done.1 = bf16[1,1,128,4096]{3,2,1,0:T(8,128)(2,1)S(1)} copy-done((bf16[1,1,128,4096]{3,2,1,0:T(8,128)(2,1)S(1)}, bf16[1,1,128,4096]{3,2,1,0:T(8,128)(2,1)}, u32[]{:S(2)}) %copy-start.1) | copy-done | bytes 1048600
  3.8 0.0 copy-start.2
  3.8 0.9 %copy-done.2 = bf16[1,1,128,512]{3,2,1,0:T(8,128)(2,1)S(1)} copy-done((bf16[1,1,128,512]{3,2,1,0:T(8,128)(2,1)S(1)}, bf16[1,1,128,512]{3,2,1,0:T(8,128)(2,1)}, u32[]{:S(2)}) %copy-start.2) | copy-done | bytes 131096
  4.7 0.0 copy-start.3
  4.7 0.9 %copy-done.3 = bf16[1,1,128,512]{3,2,1,0:T(8,128)(2,1)S(1)} copy-done((bf16[1,1,128,512]{3,2,1,0:T(8,128)(2,1)S(1)}, bf16[1,1,128,512]{3,2,1,0:T(8,128)(2,1)}, u32[]{:S(2)}) %copy-start.3) | copy-done | bytes 131096
  5.6 34.8 %shard_map.84 = (bf16[128,4096]{1,0:T(8,128)(2,1)S(1)}, bf16[128,512]{1,0:T(8,128)(2,1)S(1)}, bf16[128,512]{1,0:T(8,128)(2,1)S(1)}, f32[1,5120]{1,0:T(1,128)S(1)}) custom-call(bf16[128,4096]{1,0:T(8,128)(2,1)S(1)} %bitcast.7, bf16[128,512]{1,0:T(8,128)(2,1)S(1)} %bitcast.10, bf16[128,512]{1,0:T(8,128)(2,1)S(1)} %bitcast.11, bf16[128,4096]{1,0:T(8,128)(2,1)S(1)} %bitcast.8, ...), custom_call_target="tpu_custom_call" | custom-call | tf_op jit(solution)/shard_map/pallas_call | solution.py:269
  40.4 1.0 %copy.13 = bf16[1,1,128,4096]{3,2,1,0:T(8,128)(2,1)} copy(bf16[1,1,128,4096]{3,2,1,0:T(8,128)(2,1)S(1)} %bitcast.9) | data formatting | bytes 2097152
  41.4 0.7 %copy.14 = bf16[1,1,128,512]{3,2,1,0:T(8,128)(2,1)} copy(bf16[1,1,128,512]{3,2,1,0:T(8,128)(2,1)S(1)} %bitcast.13) | data formatting | bytes 262144
  42.0 0.7 %copy.15 = bf16[1,1,128,512]{3,2,1,0:T(8,128)(2,1)} copy(bf16[1,1,128,512]{3,2,1,0:T(8,128)(2,1)S(1)} %bitcast.12) | data formatting | bytes 262144
  42.7 0.6 %copy.16 = f32[1,5120]{1,0:T(1,128)} copy(f32[1,5120]{1,0:T(1,128)S(1)} %get-tuple-element.19) | data formatting | bytes 40960
Async XLA Ops:
  0.6 0.7 %copy-start.4 = (s32[1,256]{1,0:T(1,128)S(1)}, s32[1,256]{1,0:T(1,128)}, u32[]{:S(2)}) copy-start(s32[1,256]{1,0:T(1,128)} %seg_hbm.1) | copy-start | bytes 3076
  1.3 1.2 %copy-start = (bf16[1,1,128,4096]{3,2,1,0:T(8,128)(2,1)S(1)}, bf16[1,1,128,4096]{3,2,1,0:T(8,128)(2,1)}, u32[]{:S(2)}) copy-start(bf16[1,1,128,4096]{3,2,1,0:T(8,128)(2,1)} %param.5) | copy-start | bytes 3145732
  2.5 1.2 %copy-start.1 = (bf16[1,1,128,4096]{3,2,1,0:T(8,128)(2,1)S(1)}, bf16[1,1,128,4096]{3,2,1,0:T(8,128)(2,1)}, u32[]{:S(2)}) copy-start(bf16[1,1,128,4096]{3,2,1,0:T(8,128)(2,1)} %param.8) | copy-start | bytes 3145732
  3.8 0.9 %copy-start.2 = (bf16[1,1,128,512]{3,2,1,0:T(8,128)(2,1)S(1)}, bf16[1,1,128,512]{3,2,1,0:T(8,128)(2,1)}, u32[]{:S(2)}) copy-start(bf16[1,1,128,512]{3,2,1,0:T(8,128)(2,1)} %param.6) | copy-start | bytes 393220
  4.7 0.9 %copy-start.3 = (bf16[1,1,128,512]{3,2,1,0:T(8,128)(2,1)S(1)}, bf16[1,1,128,512]{3,2,1,0:T(8,128)(2,1)}, u32[]{:S(2)}) copy-start(bf16[1,1,128,512]{3,2,1,0:T(8,128)(2,1)} %param.7) | copy-start | bytes 393220

commit v2 on v1

--- a/solution.py
+++ b/solution.py
@@ -12,11 +12,12 @@
 SHARED_GROUPS = 4
 FEATURE_SIZE = 128
 QUERY_PER_KEY = 8
-HALF = 4
+PAIR = 2
 BIAS_ROWS = 16
 MESH = pl.DeviceIdType.MESH
 F32 = jnp.float32
 BF16 = jnp.bfloat16
+VMEM_GRANT = 62 * 1024 * 1024
 
 
 def dot(a, b, a_dim, b_dim):
@@ -80,10 +81,10 @@
             device_id=ahead(r), device_id_type=MESH,
         )
 
-    def back_copy(g, r):
+    def back_copy(g, r, i):
         return pltpu.make_async_remote_copy(
-            src_ref=back_out.at[g, r - 1], dst_ref=back_in.at[g, r - 1],
-            send_sem=back_send.at[g, r - 1], recv_sem=back_recv.at[g, r - 1],
+            src_ref=back_out.at[g, r - 1, i], dst_ref=back_in.at[g, r - 1, i],
+            send_sem=back_send.at[g, r - 1, i], recv_sem=back_recv.at[g, r - 1, i],
             device_id=behind(r), device_id_type=MESH,
         )
 
@@ -118,13 +119,13 @@
 
     pl.semaphore_wait(barrier, len(greeted))
 
+    @pl.loop(0, ASKER_STREAMS)
+    def _(h):
+        cot_copy(h).start()
+
     for r in range(1, reach + 1):
         for i in range(2):
             halo_copy(i, r).start()
-
-    @pl.loop(0, ASKER_STREAMS)
-    def _(h):
-        cot_copy(h).start()
 
     seg_copy.wait()
     query_doc = seg[:, pl.ds(pl.multiple_of(my_ctx * rows, rows), rows)].astype(F32)
@@ -159,72 +160,79 @@
             weights = jnp.exp2(scores - jnp.max(scores, axis=0, keepdims=True))
             probs[h] = weights * (1.0 / jnp.sum(weights, axis=0, keepdims=True))
 
+    def send_back(g, i, grad):
+        for r in range(1, reach + 1):
+            part = slice((reach - r) * rows, (reach - r + 1) * rows)
+            back_out[g, r - 1, i] = grad[part].astype(BF16)
+            back_copy(g, r, i).start()
+
+    def wait_sent(g):
+        for i in range(QUERY_PER_KEY):
+            cot_copy(g * QUERY_PER_KEY + i).wait_send()
+            dq_copy(g * QUERY_PER_KEY + i).wait()
+        for r in range(1, reach + 1):
+            for i in range(2):
+                back_copy(g, r, i).wait_send()
+        if in_kernel_sum:
+            for i in range(len(offsets)):
+                bias_copy(g, i).wait_send()
+
     @pl.loop(0, SHARED_GROUPS)
     def _(g):
         key_block = keys[:, columns(g)]
         value_block = values[:, columns(g)]
-        for half in range(QUERY_PER_KEY // HALF):
-            first = g * QUERY_PER_KEY + half * HALF
-            grads, probs_b = [], []
-            for i in range(HALF):
+        for pair in range(QUERY_PER_KEY // PAIR):
+            last = pair == QUERY_PER_KEY // PAIR - 1
+            first = g * QUERY_PER_KEY + pair * PAIR
+            these = pl.ds(pl.multiple_of(first * rows, rows), PAIR * rows)
+            grads = []
+            for i in range(PAIR):
                 h = first + i
                 cot_copy(h).wait_recv()
+                if i == PAIR - 1:
+                    probs_b = jnp.concatenate(
+                        [probs[first + n].astype(BF16) for n in range(PAIR)], axis=1
+                    )
+                    dv = dot(probs_b, cot_rows[these, :], 1, 0)
+                    if pair:
+                        dv = acc[g, 1] + dv
+                    acc[g, 1] = dv
+                    if last:
+                        send_back(g, 1, dv)
                 p = probs[h]
-                pb = p.astype(BF16)
                 grad_prob = dot(value_block, cot_rows[head_rows(h), :], 1, 1)
-                dot_out = jnp.sum(pb.astype(F32) * grad_prob, axis=0, keepdims=True)
+                dot_out = jnp.sum(p.astype(BF16).astype(F32) * grad_prob, axis=0, keepdims=True)
                 grads.append((p * (grad_prob - dot_out) * scaling).astype(BF16))
-                probs_b.append(pb)
             grads = jnp.concatenate(grads, axis=1)
-            probs_b = jnp.concatenate(probs_b, axis=1)
-            these = pl.ds(pl.multiple_of(first * rows, rows), HALF * rows)
             dk = dot(grads, q_rows[these, :], 1, 0)
-            dv = dot(probs_b, cot_rows[these, :], 1, 0)
-            if half:
+            if pair:
                 dk = acc[g, 0] + dk
-                dv = acc[g, 1] + dv
             acc[g, 0] = dk
-            acc[g, 1] = dv
-            if half == QUERY_PER_KEY // HALF - 1:
-                for r in range(1, reach + 1):
-                    part = slice((reach - r) * rows, (reach - r + 1) * rows)
-                    back_out[g, r - 1, 0] = dk[part].astype(BF16)
-                    back_out[g, r - 1, 1] = dv[part].astype(BF16)
-                    back_copy(g, r).start()
-                bias_mine[g, 8:9, :] = jnp.sum(dk, axis=0, keepdims=True)
-                bias_mine[g, 9:10, :] = jnp.sum(dv, axis=0, keepdims=True)
+            if last:
+                send_back(g, 0, dk)
             dq = dot(grads, key_block, 0, 0)
-            dq_rows[these, :] = dq.astype(BF16)
-            for i in range(HALF):
-                row = half * HALF + i
+            for i in range(PAIR):
+                row = pair * PAIR + i
                 bias_mine[g, row : row + 1, :] = jnp.sum(
                     dq[i * rows : (i + 1) * rows], axis=0, keepdims=True
                 )
+            if last:
+                bias_mine[g, 8:9, :] = jnp.sum(dk, axis=0, keepdims=True)
+                bias_mine[g, 9:10, :] = jnp.sum(dv, axis=0, keepdims=True)
+                if in_kernel_sum:
+                    for i in range(len(offsets)):
+                        bias_copy(g, i).start()
+            dq_rows[these, :] = dq.astype(BF16)
+            for i in range(PAIR):
                 dq_copy(first + i).start()
-        if in_kernel_sum:
-            for i in range(len(offsets)):
-                bias_copy(g, i).start()
-
-    for g in range(SHARED_GROUPS):
-        part = pl.ds(g * width, width)
-        dk = acc[g, 0, pl.ds(reach * rows, rows), :]
-        dv = acc[g, 1, pl.ds(reach * rows, rows), :]
-        for r in range(1, reach + 1):
-            back_copy(g, r).wait_recv()
-            dk = dk + back_in[g, r - 1, 0].astype(F32)
-            dv = dv + back_in[g, r - 1, 1].astype(F32)
-        dk_out[:, part] = dk.astype(BF16)
-        dv_out[:, part] = dv.astype(BF16)
-    outs = [
-        pltpu.make_async_copy(dk_out, dk_hbm, out_sem.at[0]),
-        pltpu.make_async_copy(dv_out, dv_hbm, out_sem.at[1]),
-        pltpu.make_async_copy(bias_out, bias_hbm, out_sem.at[2]),
-    ]
-    outs[0].start()
-    outs[1].start()
+
+        @pl.when(g > 0)
+        def _():
+            wait_sent(g - 1)
 
     bias_scale = 1.0 / math.sqrt(dp * length)
-    for g in range(SHARED_GROUPS):
+
+    def finish_bias(g):
         total = bias_mine[g]
         if in_kernel_sum:
             for i in range(len(offsets)):
@@ -235,25 +243,56 @@
             bias_out[:, pl.ds((g * QUERY_PER_KEY + i) * width, width)] = total[i : i + 1, :]
         bias_out[:, pl.ds((ASKER_STREAMS + g) * width, width)] = total[8:9, :]
         bias_out[:, pl.ds((ASKER_STREAMS + SHARED_GROUPS + g) * width, width)] = total[9:10, :]
+
+    def finish_kv(g, i, out):
+        total = acc[g, i, pl.ds(reach * rows, rows), :]
+        for r in range(1, reach + 1):
+            back_copy(g, r, i).wait_recv()
+            total = total + back_in[g, r - 1, i].astype(F32)
+        out[:, pl.ds(g * width, width)] = total.astype(BF16)
+
+    outs = [
+        pltpu.make_async_copy(dk_out, dk_hbm, out_sem.at[0]),
+        pltpu.make_async_copy(dv_out, dv_hbm, out_sem.at[1]),
+        pltpu.make_async_copy(bias_out, bias_hbm, out_sem.at[2]),
+    ]
+    for g in range(SHARED_GROUPS):
+        finish_kv(g, 1, dv_out)
+        if g < SHARED_GROUPS - 1:
+            finish_bias(g)
+            finish_kv(g, 0, dk_out)
+    outs[1].start()
+    finish_kv(SHARED_GROUPS - 1, 0, dk_out)
+    outs[0].start()
+    finish_bias(SHARED_GROUPS - 1)
     outs[2].start()
 
     for r in range(1, reach + 1):
         for i in range(2):
             halo_copy(i, r).wait_send()
-        for g in range(SHARED_GROUPS):
-            back_copy(g, r).wait_send()
-    if in_kernel_sum:
-        for i in range(len(offsets)):
-            for g in range(SHARED_GROUPS):
-                bias_copy(g, i).wait_send()
-
-    @pl.loop(0, ASKER_STREAMS)
-    def _(h):
-        cot_copy(h).wait_send()
-        dq_copy(h).wait()
-
+    wait_sent(SHARED_GROUPS - 1)
     for copy in outs:
         copy.wait()
+
+
+def write_out(*refs):
+    count = len(refs) // 3
+    ins, outs, held = refs[:count], refs[count : 2 * count], refs[2 * count : 3 * count]
+    in_sem, out_sem = refs[3 * count :]
+    parts = [(0, pl.ds(n * 32, 32)) for n in range(ins[0].shape[0] // 32)]
+    parts += [(i, slice(None)) for i in range(1, count)]
+
+    def copy(n, source, target, sem):
+        i, part = parts[n]
+        return pltpu.make_async_copy(source[i].at[part], target[i].at[part], sem.at[n])
+
+    for n in range(len(parts)):
+        copy(n, ins, held, in_sem).start()
+    for n in range(len(parts)):
+        copy(n, ins, held, in_sem).wait()
+        copy(n, held, outs, out_sem).start()
+    for n in range(len(parts)):
+        copy(n, held, outs, out_sem).wait()
 
 
 def body(pipe, ctx, dp, queries, key_input, value_input, incoming, segments):
@@ -266,14 +305,15 @@
     q_width = ASKER_STREAMS * FEATURE_SIZE
     kv_width = SHARED_GROUPS * FEATURE_SIZE
     dma = pltpu.SemaphoreType.DMA
-    dq, dk, dv, bias = pl.pallas_call(
+    shapes = (
+        jax.ShapeDtypeStruct((rows, q_width), BF16),
+        jax.ShapeDtypeStruct((rows, kv_width), BF16),
+        jax.ShapeDtypeStruct((rows, kv_width), BF16),
+        jax.ShapeDtypeStruct((1, q_width + 2 * kv_width), F32),
+    )
+    results = pl.pallas_call(
         functools.partial(kernel, (pipe, ctx, dp, reach), in_kernel_sum),
-        out_shape=(
-            jax.ShapeDtypeStruct((rows, q_width), BF16),
-            jax.ShapeDtypeStruct((rows, kv_width), BF16),
-            jax.ShapeDtypeStruct((rows, kv_width), BF16),
-            jax.ShapeDtypeStruct((1, q_width + 2 * kv_width), F32),
-        ),
+        out_shape=shapes,
         in_specs=[pl.BlockSpec(memory_space=pl.ANY)] * 5,
         out_specs=[pl.BlockSpec(memory_space=pl.ANY)] * 4,
         scratch_shapes=[
@@ -300,17 +340,25 @@
             dma((2, reach)),
             dma((2, reach)),
             dma,
-            dma((SHARED_GROUPS, reach)),
-            dma((SHARED_GROUPS, reach)),
+            dma((SHARED_GROUPS, reach, 2)),
+            dma((SHARED_GROUPS, reach, 2)),
             dma((peers, SHARED_GROUPS)),
             dma((peers, SHARED_GROUPS)),
             dma((ASKER_STREAMS,)),
             dma((3,)),
         ],
         compiler_params=pltpu.CompilerParams(
-            collective_id=0, has_side_effects=True, vmem_limit_bytes=48 * 1024 * 1024
+            collective_id=0, has_side_effects=True, vmem_limit_bytes=VMEM_GRANT
         ),
     )(queries[0, 0], key_input[0, 0], value_input[0, 0], incoming[0, 0], segments)
+    dq, dk, dv, bias = pl.pallas_call(
+        write_out,
+        out_shape=shapes,
+        in_specs=[pl.BlockSpec(memory_space=pl.ANY)] * 4,
+        out_specs=[pl.BlockSpec(memory_space=pl.ANY)] * 4,
+        scratch_shapes=[pltpu.VMEM(shape.shape, shape.dtype) for shape in shapes]
+        + [dma((rows // 32 + 3,)), dma((rows // 32 + 3,))],
+    )(*results)
     if not in_kernel_sum:
         bias = lax.psum(bias, ("ctx", "dp"))
     return dq[None, None], dk[None, None], dv[None, None], bias

time: 43.6 us -> 37.9 us (0.87)
  local copies, waits for them, and re-layouts: 7.82 us -> 0 us
  Pallas kernels: 34.8 us -> 37.1 us
    unnamed x14 -> x0, local copies, waits for them, and re-layouts: 7.82 us -> none
    pallas_call x0 -> x1, Pallas kernels: none -> 2.12 us  [body(): pl.pallas_call(write_out, out_shape=shapes, in_specs=[pl.BlockSpec(memory...]
where the time goes in v2:
time: 37.9 us; the launch traced here: 37.8 us
  Pallas kernels  37.1 us (98%)
  between operations  0.64 us (2%)
    pallas_call x1, Pallas kernels, body(): pl.pallas_call(functools.partial(kernel, (pipe, ctx, dp, reach), in_kerne...  35 us
    pallas_call x1, Pallas kernels, body(): pl.pallas_call(write_out, out_shape=shapes, in_specs=[pl.BlockSpec(memory...  2.12 us

profile of v2, /device:TPU:0, one launch (start us, length us, event | category | flops | bytes accessed | tf_op | source)
XLA Modules:
  0.0 37.8 jit_solution(11402540898618166611)
XLA Ops:
  0.6 35.0 %shard_map.84 = (bf16[128,4096]{1,0:T(8,128)(2,1)}, bf16[128,512]{1,0:T(8,128)(2,1)}, bf16[128,512]{1,0:T(8,128)(2,1)}, f32[1,5120]{1,0:T(1,128)}) custom-call(bf16[128,4096]{1,0:T(8,128)(2,1)} %bitcast.7, bf16[128,512]{1,0:T(8,128)(2,1)} %bitcast.9, bf16[128,512]{1,0:T(8,128)(2,1)} %bitcast.10, bf16[128,4096]{1,0:T(8,128)(2,1)} %bitcast.8, s32[1,256]{1,0:T(1,128)} %seg_hbm.1), custom_call_target="tpu_custom_call" | custom-call | tf_op jit(solution)/shard_map/pallas_call | solution.py:314
  35.6 2.1 %shard_map.85 = (bf16[128,4096]{1,0:T(8,128)(2,1)}, bf16[128,512]{1,0:T(8,128)(2,1)}, bf16[128,512]{1,0:T(8,128)(2,1)}, f32[1,5120]{1,0:T(1,128)}) custom-call(bf16[128,4096]{1,0:T(8,128)(2,1)} %get-tuple-element.12.refs_0_, bf16[128,512]{1,0:T(8,128)(2,1)} %get-tuple-element.13.refs_1_, bf16[128,512]{1,0:T(8,128)(2,1)} %get-tuple-element.14.refs_2_, ...), custom_call_target="tpu_custom_call" | custom-call | tf_op jit(solution)/shard_map/pallas_call | solution.py:354
